TPU v7x, 32 devices: a whole 2x2x4 slice. The times are simulated.
32 devices in a mesh: dp: 8 (over z, x), mp: 4 (over y, core).
Axes of the slice: x: 2, y: 2, z: 4, core: 2. Of those that a mesh axis runs over, the one named last changes fastest.
Arguments:
- tokens: bfloat16 [49152, 1280], P(('dp', 'mp')), may hold values from -40 to 40, as said below
- lengths: int32 [768, 32], P('dp'), may hold values from 0 to 64, as said below
- cotangent: bfloat16 [49152, 1280], P(('dp', 'mp')), may hold values from -6 to 6
- query_weight: bfloat16 [1280, 1280], P(None, 'mp'), may hold values from -0.15625 to 0.15625
- key_weight: bfloat16 [1280, 1280], P(None, 'mp'), may hold values from -0.15625 to 0.15625
- value_weight: bfloat16 [1280, 1280], P(None, 'mp'), may hold values from -0.15625 to 0.15625
- out_weight: bfloat16 [1280, 1280], P('mp'), may hold values from -0.3125 to 0.3125
- up_weight: bfloat16 [1280, 5120], P(None, 'mp'), may hold values from -0.15625 to 0.15625
- hidden_bias: bfloat16 [5120], P('mp'), may hold values from -3 to 3
- down_weight: bfloat16 [5120, 1280], P('mp'), may hold values from -0.078125 to 0.078125
- output_bias: bfloat16 [1280], replicated, may hold values from -2 to 2
- first_gain: bfloat16 [1280], replicated, may hold values from 0.099609375 to 1.8984375
- second_gain: bfloat16 [1280], replicated, may hold values from 0.099609375 to 1.8984375
Outputs:
- layer_output: bfloat16 [49152, 1280], P(('dp', 'mp'))
- input_gradient: float32 [49152, 1280], P(('dp', 'mp'))
- query_gradient: float32 [1280, 1280], P(None, 'mp')
- key_gradient: float32 [1280, 1280], P(None, 'mp')
- value_gradient: float32 [1280, 1280], P(None, 'mp')
- out_gradient: float32 [1280, 1280], P('mp')
- up_gradient: float32 [1280, 5120], P(None, 'mp')
- hidden_bias_gradient: float32 [5120], P('mp')
- down_gradient: float32 [5120, 1280], P('mp')
- output_bias_gradient: float32 [1280], replicated
- first_gain_gradient: float32 [1280], replicated
- second_gain_gradient: float32 [1280], replicated
- rms_stats: float32 [3], replicated
Inputs may be any that keep to these rules, and one draw needn't show every extreme that they name: Each row lists the lengths of the series packed into it in order, zeros only after the last; every row holds one series or more and at most 64 patches; some row holds a single series of 64. `tokens`: activations of order one.
All inputs are finite; a program needn't handle non-finite values.
Results may differ from a plain program's by a relative error of at most 0.018.
Values may be sent and summed in bfloat16 or wider, within the bound.
A program may use at most 384 MiB of HBM per device.

v0:
```python
import math
import jax
import jax.numpy as jnp
from jax import lax
from jax.sharding import PartitionSpec as P

D = 1280
HD = 80
L = 64
SLOTS = 32
EPSILON = 1e-06
MASKED_SCORE = -1e30


def segments(lengths):
    ends = jnp.cumsum(lengths, axis=1)
    places = lax.broadcasted_iota(jnp.int32, (lengths.shape[0], L, lengths.shape[1]), 1)
    return jnp.sum((ends[:, None, :] <= places).astype(jnp.int32), axis=2)


def normalize(values, gain):
    scale_rows = lax.rsqrt(jnp.mean(values * values, axis=1, keepdims=True) + EPSILON)
    normed = (values * scale_rows * gain.astype(jnp.float32)).astype(jnp.bfloat16)
    return (scale_rows, normed)


def norm_back(values, scale_rows, gain, grad):
    weighted = gain.astype(jnp.float32) * grad
    inner = jnp.sum(weighted * values, axis=1, keepdims=True)
    gain_part = jnp.sum(grad * values * scale_rows, axis=0)
    back = (
        weighted * scale_rows
        - values * scale_rows * scale_rows * scale_rows * inner / values.shape[1]
    )
    return (gain_part, back)


def per_device(
    tokens,
    lengths,
    cotangent,
    query_weight,
    key_weight,
    value_weight,
    out_weight,
    up_weight,
    hidden_bias,
    down_weight,
    output_bias,
    first_gain,
    second_gain,
):
    local_rows = tokens.shape[0]
    width = query_weight.shape[1]
    heads_here = width // HD
    rows_here = lengths.shape[0]
    scale = 1.0 / math.sqrt(HD)
    segment_ids = segments(lengths)
    valid_all = (segment_ids < SLOTS).reshape(-1).astype(jnp.float32)
    valid = lax.dynamic_slice_in_dim(valid_all, lax.axis_index("mp") * local_rows, local_rows)
    causal = lax.broadcasted_iota(jnp.int32, (L, L), 1) <= lax.broadcasted_iota(
        jnp.int32, (L, L), 0
    )
    allowed = ((segment_ids[:, :, None] == segment_ids[:, None, :]) & causal[None])[:, None]
    inputs = tokens.astype(jnp.float32)
    first_scale, first_normed = normalize(inputs, first_gain)
    first_rows = lax.all_gather(first_normed, "mp", axis=0, tiled=True)
    joined_weight = jnp.concatenate([query_weight, key_weight, value_weight], axis=1)
    joined = jnp.dot(first_rows, joined_weight, preferred_element_type=jnp.float32).astype(
        jnp.bfloat16
    )
    queries = joined[:, :width].reshape(rows_here, L, heads_here, HD)
    keys = joined[:, width : 2 * width].reshape(rows_here, L, heads_here, HD)
    values = joined[:, 2 * width :].reshape(rows_here, L, heads_here, HD)

    def masked_scores():
        scores = (
            jnp.einsum("rqhe,rkhe->rhqk", queries, keys, preferred_element_type=jnp.float32) * scale
        )
        return jnp.where(allowed, scores, MASKED_SCORE)

    scores = masked_scores()
    peak = jnp.max(scores, axis=-1, keepdims=True)
    logsum = peak + jnp.log(jnp.sum(jnp.exp(scores - peak), axis=-1, keepdims=True))
    probs_low = jnp.exp(scores - logsum).astype(jnp.bfloat16)
    mixed = jnp.einsum("rhqk,rkhe->rqhe", probs_low, values, preferred_element_type=jnp.float32)
    mixed = mixed.astype(jnp.bfloat16).reshape(rows_here * L, width)
    attention_local = lax.psum_scatter(
        jnp.dot(mixed, out_weight, preferred_element_type=jnp.float32).astype(jnp.bfloat16),
        "mp",
        scatter_dimension=0,
        tiled=True,
    ).astype(jnp.float32)
    hidden = inputs + attention_local
    second_scale, second_normed = normalize(hidden, second_gain)
    second_rows = lax.all_gather(second_normed, "mp", axis=0, tiled=True)
    preact = jnp.dot(
        second_rows, up_weight, preferred_element_type=jnp.float32
    ) + hidden_bias.astype(jnp.float32)
    sigma = jax.nn.sigmoid(preact)
    active = (preact * sigma).astype(jnp.bfloat16)
    feed_local = lax.psum_scatter(
        jnp.dot(active, down_weight, preferred_element_type=jnp.float32).astype(jnp.bfloat16),
        "mp",
        scatter_dimension=0,
        tiled=True,
    ).astype(jnp.float32) + output_bias.astype(jnp.float32)
    result = hidden + feed_local
    mask_col = valid[:, None]
    squares = jnp.stack(
        [
            jnp.sum(mask_col * attention_local * attention_local),
            jnp.sum(mask_col * feed_local * feed_local),
            jnp.sum(mask_col * result * result),
        ]
    )
    count = jnp.sum(valid)
    grad_out = cotangent.astype(jnp.float32)
    output_bias_part = jnp.sum(grad_out, axis=0)
    grad_rows = lax.all_gather(cotangent, "mp", axis=0, tiled=True)
    down_part = jnp.einsum("tf,td->fd", active, grad_rows, preferred_element_type=jnp.float32)
    active_grad = jnp.einsum(
        "td,fd->tf", grad_rows, down_weight, preferred_element_type=jnp.float32
    )
    active_grad = active_grad.astype(jnp.bfloat16).astype(jnp.float32)
    preact_grad = (active_grad * (sigma + preact * sigma * (1.0 - sigma))).astype(jnp.bfloat16)
    bias_part = jnp.sum(preact_grad.astype(jnp.float32), axis=0)
    up_part = jnp.einsum("td,tf->df", second_rows, preact_grad, preferred_element_type=jnp.float32)
    second_grad = lax.psum_scatter(
        jnp.einsum("tf,df->td", preact_grad, up_weight, preferred_element_type=jnp.float32).astype(
            jnp.bfloat16
        ),
        "mp",
        scatter_dimension=0,
        tiled=True,
    ).astype(jnp.float32)
    second_gain_part, second_back = norm_back(hidden, second_scale, second_gain, second_grad)
    hidden_grad = grad_out + second_back
    branch_low = hidden_grad.astype(jnp.bfloat16)
    branch_grad = lax.all_gather(branch_low, "mp", axis=0, tiled=True)
    out_part = jnp.einsum("tk,td->kd", mixed, branch_grad, preferred_element_type=jnp.float32)
    mixed_grad = jnp.einsum(
        "td,kd->tk", branch_grad, out_weight, preferred_element_type=jnp.float32
    )
    mixed_grad = mixed_grad.astype(jnp.bfloat16).reshape(rows_here, L, heads_here, HD)
    probs = jnp.exp(masked_scores() - logsum)
    probs_grad = jnp.einsum(
        "rqhe,rkhe->rhqk", mixed_grad, values, preferred_element_type=jnp.float32
    )
    value_grad = jnp.einsum(
        "rhqk,rqhe->rkhe",
        probs.astype(jnp.bfloat16),
        mixed_grad,
        preferred_element_type=jnp.float32,
    ).astype(jnp.bfloat16)
    inner = jnp.sum(probs * probs_grad, axis=-1, keepdims=True)
    scores_grad = (probs * (probs_grad - inner)).astype(jnp.bfloat16)
    query_grad = (
        jnp.einsum("rhqk,rkhe->rqhe", scores_grad, keys, preferred_element_type=jnp.float32) * scale
    ).astype(jnp.bfloat16)
    key_grad = (
        jnp.einsum("rhqk,rqhe->rkhe", scores_grad, queries, preferred_element_type=jnp.float32)
        * scale
    ).astype(jnp.bfloat16)
    joined_grad = jnp.concatenate(
        [
            query_grad.reshape(rows_here * L, width),
            key_grad.reshape(rows_here * L, width),
            value_grad.reshape(rows_here * L, width),
        ],
        axis=1,
    )
    joined_part = jnp.einsum(
        "td,tk->dk", first_rows, joined_grad, preferred_element_type=jnp.float32
    )
    query_part = joined_part[:, :width]
    key_part = joined_part[:, width : 2 * width]
    value_part = joined_part[:, 2 * width :]
    first_grad = lax.psum_scatter(
        jnp.einsum(
            "tk,dk->td", joined_grad, joined_weight, preferred_element_type=jnp.float32
        ).astype(jnp.bfloat16),
        "mp",
        scatter_dimension=0,
        tiled=True,
    ).astype(jnp.float32)
    first_gain_part, first_back = norm_back(inputs, first_scale, first_gain, first_grad)
    input_gradient = hidden_grad + first_back
    query_total, key_total, value_total, out_total, up_total, bias_total, down_total = (
        lax.psum(query_part.astype(jnp.bfloat16), "dp").astype(jnp.float32),
        lax.psum(key_part.astype(jnp.bfloat16), "dp").astype(jnp.float32),
        lax.psum(value_part.astype(jnp.bfloat16), "dp").astype(jnp.float32),
        lax.psum(out_part.astype(jnp.bfloat16), "dp").astype(jnp.float32),
        lax.psum(up_part.astype(jnp.bfloat16), "dp").astype(jnp.float32),
        lax.psum(bias_part.astype(jnp.bfloat16), "dp").astype(jnp.float32),
        lax.psum(down_part.astype(jnp.bfloat16), "dp").astype(jnp.float32),
    )
    first_total, second_total, output_bias_total, squares_total, count_total = lax.psum(
        (first_gain_part, second_gain_part, output_bias_part, squares, count), ("dp", "mp")
    )
    rms_stats = jnp.sqrt(squares_total / (count_total * D))
    return (
        result.astype(jnp.bfloat16),
        input_gradient,
        query_total,
        key_total,
        value_total,
        out_total,
        up_total,
        bias_total,
        down_total,
        output_bias_total,
        first_total,
        second_total,
        rms_stats,
    )


def solution(mesh):
    return jax.shard_map(
        per_device,
        mesh=mesh,
        in_specs=(
            P(("dp", "mp"), None),
            P("dp", None),
            P(("dp", "mp"), None),
            P(None, "mp"),
            P(None, "mp"),
            P(None, "mp"),
            P("mp", None),
            P(None, "mp"),
            P("mp"),
            P("mp", None),
            P(),
            P(),
            P(),
        ),
        out_specs=(
            P(("dp", "mp"), None),
            P(("dp", "mp"), None),
            P(None, "mp"),
            P(None, "mp"),
            P(None, "mp"),
            P("mp", None),
            P(None, "mp"),
            P("mp"),
            P("mp", None),
            P(),
            P(),
            P(),
            P(),
        ),
        check_vma=False,
    )
```

profile of v0, /device:TPU:0, one launch (start us, length us, event | category | flops | bytes accessed | tf_op | source)
XLA Modules:
  0.0 1699.2 jit_solution(6496326896694240132)
XLA Ops:
  26.5 93.2 %all-gather.5.cloned.1.call-done = bf16[6144,1280]{1,0:T(8,128)(2,1)} async-done(((bf16[1536,1280]{1,0:T(8,128)(2,1)}), bf16[6144,1280]{1,0:T(8,128)(2,1)}) %all-gather.5.cloned.1.call-update) | async-done | bytes 15728656 | tf_op jit(solution)/shard_map/all_gather | solution.py:67
  119.6 19.1 %convolution_convert_fusion.5 = bf16[6144,960]{0,1:T(8,128)(2,1)S(1)} fusion(bf16[6144,1280]{1,0:T(8,128)(2,1)} %all-gather.5.cloned.1.call-done, bf16[1280,960]{0,1:T(8,128)(2,1)} %constant_dynamic-update-slice_fusion), kind=kOutput, calls=%fused_computation.25 | convolution fusion | flops 15105392640 | bytes 29982720 | tf_op jit(solution)/shard_map/dot_general | solution.py:69
  243.6 18.3 %copy.67 = bf16[96,64,4,80]{3,2,1,0:T(4,128)(2,1)} copy(bf16[96,64,4,80]{3,1,2,0:T(8,128)(2,1)} %convert_bitcast_fusion.1) | data formatting | bytes 7864320 | tf_op jit(solution)/shard_map/convert_element_type | solution.py:87
  286.9 119.3 %reduce-scatter.5.cloned.1.call-done = bf16[1536,1280]{1,0:T(8,128)(2,1)} async-done(((bf16[6144,1280]{1,0:T(8,128)(2,1)}), bf16[1536,1280]{1,0:T(8,128)(2,1)}) %reduce-scatter.5.cloned.1.call-update) | async-done | bytes 3932176 | tf_op jit(solution)/shard_map/reduce_scatter | solution.py:88
  415.6 99.5 %all-gather.7.cloned.1.call-done = bf16[6144,1280]{1,0:T(8,128)(2,1)} async-done(((bf16[1536,1280]{1,0:T(8,128)(2,1)}), bf16[6144,1280]{1,0:T(8,128)(2,1)}) %all-gather.7.cloned.1.call-update) | async-done | bytes 15728656 | tf_op jit(solution)/shard_map/all_gather | solution.py:96
  515.1 32.9 %fusion = (bf16[6144,1280]{1,0:T(8,128)(2,1)}, f32[6144,1280]{1,0:T(8,128)}) fusion(f32[1280]{0:T(1024)S(1)} %convert_element_type.161, bf16[6144,1280]{1,0:T(8,128)(2,1)} %all-gather.7.cloned.1.call-done, bf16[1280,1280]{1,0:T(8,128)(2,1)S(1)} %copy-done), kind=kOutput, calls=%fused_computation.3 | convolution fusion | flops 20179845120 | bytes 66196480 | tf_op jit(solution)/shard_map/dot_general | solution.py:97
  547.9 25.9 %convolution_convert_fusion.2 = bf16[6144,1280]{1,0:T(8,128)(2,1)} fusion(bf16[6144,1280]{1,0:T(8,128)(2,1)} %get-tuple-element.44, bf16[1280,1280]{1,0:T(8,128)(2,1)S(1)} %copy-done.38), kind=kOutput, calls=%fused_computation.6 | convolution fusion | flops 20140523520 | bytes 34734080 | tf_op jit(solution)/shard_map/dot_general | solution.py:103
  573.9 42.6 %all-gather.9.cloned.1.call-done = bf16[6144,1280]{1,0:T(8,128)(2,1)} async-done(((bf16[1536,1280]{1,0:T(8,128)(2,1)}), bf16[6144,1280]{1,0:T(8,128)(2,1)}) %all-gather.9.cloned.1.call-update) | async-done | bytes 15728656 | tf_op jit(solution)/shard_map/all_gather | solution.py:120
  616.5 38.5 %fusion.39 = (bf16[1280]{0:T(1024)(128)(2,1)}, bf16[6144,1280]{1,0:T(8,128)(2,1)}) fusion(f32[6144,1280]{1,0:T(8,128)} %get-tuple-element.45, f32[1280]{0:T(1024)S(1)} %convert_element_type.161, bf16[6144,1280]{1,0:T(8,128)(2,1)} %all-gather.9.cloned.1.call-done, bf16[1280,1280]{1,0:T(8,128)(2,1)} %param.22), kind=kOutput, calls=%fused_computation.89 | convolution fusion | flops 20234893312 | bytes 66199040 | tf_op jit(solution)/shard_map/td,fd->tf/dot_general | solution.py:122
  655.0 25.9 %convolution_convert_fusion = bf16[6144,1280]{1,0:T(8,128)(2,1)} fusion(bf16[6144,1280]{1,0:T(8,128)(2,1)} %get-tuple-element.49, bf16[1280,1280]{1,0:T(8,128)(2,1)S(1)} %copy-done), kind=kOutput, calls=%fused_computation.4 | convolution fusion | flops 20140523520 | bytes 34734080 | tf_op jit(solution)/shard_map/tf,df->td/dot_general | solution.py:130
  682.5 56.3 %reduce-scatter.7.cloned.1.call-done = bf16[1536,1280]{1,0:T(8,128)(2,1)} async-done(((bf16[6144,1280]{1,0:T(8,128)(2,1)}), bf16[1536,1280]{1,0:T(8,128)(2,1)}) %reduce-scatter.7.cloned.1.call-update) | async-done | bytes 3932176 | tf_op jit(solution)/shard_map/reduce_scatter | solution.py:102
  738.8 122.3 %reduce-scatter.9.cloned.1.call-done = bf16[1536,1280]{1,0:T(8,128)(2,1)} async-done(((bf16[6144,1280]{1,0:T(8,128)(2,1)}), bf16[1536,1280]{1,0:T(8,128)(2,1)}) %reduce-scatter.9.cloned.1.call-update) | async-done | bytes 3932176 | tf_op jit(solution)/shard_map/reduce_scatter | solution.py:129
  880.7 26.7 %convolution_convert_fusion.7 = bf16[1280,1280]{1,0:T(8,128)(2,1)} fusion(bf16[6144,1280]{1,0:T(8,128)(2,1)} %get-tuple-element.44, bf16[6144,1280]{1,0:T(8,128)(2,1)} %all-gather.9.cloned.1.call-done), kind=kOutput, calls=%fused_computation.59 | convolution fusion | flops 20134297600 | bytes 34734080 | tf_op jit(solution)/shard_map/tf,td->fd/dot_general | solution.py:121
  907.4 26.8 %convolution_convert_fusion.8 = bf16[1280,1280]{1,0:T(8,128)(2,1)} fusion(bf16[6144,1280]{1,0:T(8,128)(2,1)} %all-gather.7.cloned.1.call-done, bf16[6144,1280]{1,0:T(8,128)(2,1)} %get-tuple-element.49), kind=kOutput, calls=%fused_computation.60 | convolution fusion | flops 20134297600 | bytes 34734080 | tf_op jit(solution)/shard_map/td,tf->df/dot_general | solution.py:128
  934.1 46.6 %all-gather.11.cloned.1.call-done = bf16[6144,1280]{1,0:T(8,128)(2,1)} async-done(((bf16[1536,1280]{1,0:T(8,128)(2,1)}), bf16[6144,1280]{1,0:T(8,128)(2,1)}) %all-gather.11.cloned.1.call-update) | async-done | bytes 15728656 | tf_op jit(solution)/shard_map/all_gather | solution.py:140
  1076.2 18.3 %copy.77 = bf16[96,64,4,80]{3,2,1,0:T(4,128)(2,1)} copy(bf16[96,64,4,80]{3,1,2,0:T(8,128)(2,1)} %convert_bitcast_fusion) | data formatting | bytes 7864320 | tf_op jit(solution)/shard_map/convert_element_type | solution.py:155
  1105.2 18.5 %copy.73 = bf16[96,64,4,80]{3,2,1,0:T(4,128)(2,1)} copy(bf16[96,64,4,80]{3,1,2,0:T(8,128)(2,1)} %fusion.26) | data formatting | bytes 7864320 | tf_op jit(solution)/shard_map/convert_element_type | solution.py:160
  1134.6 18.3 %copy.75 = bf16[96,64,4,80]{3,2,1,0:T(4,128)(2,1)} copy(bf16[96,64,4,80]{3,1,2,0:T(8,128)(2,1)} %fusion.27) | data formatting | bytes 7864320 | tf_op jit(solution)/shard_map/convert_element_type | solution.py:164
  1163.6 20.7 %fusion.30 = bf16[1280,960]{0,1:T(8,128)(2,1)S(1)} fusion(bf16[6144,1280]{1,0:T(8,128)(2,1)} %all-gather.5.cloned.1.call-done, bf16[6144,320]{1,0:T(8,128)(2,1)} %reshape.110, bf16[6144,320]{1,0:T(8,128)(2,1)} %reshape.109, bf16[6144,320]{1,0:T(8,128)(2,1)} %reshape.108), kind=kOutput, calls=%fused_computation.68 | convolution fusion | flops 15136112640 | bytes 29982720 | tf_op jit(solution)/shard_map/td,tk->dk/dot_general | solution.py:173
  1199.0 23.2 %convolution_convert_fusion.4 = bf16[6144,1280]{1,0:T(8,128)(2,1)} fusion(bf16[1280,960]{0,1:T(8,128)(2,1)} %constant_dynamic-update-slice_fusion, bf16[6144,320]{1,0:T(8,128)(2,1)} %reshape.110, bf16[6144,320]{1,0:T(8,128)(2,1)} %reshape.109, bf16[6144,320]{1,0:T(8,128)(2,1)} %reshape.108), kind=kOutput, calls=%fused_computation.8 | convolution fusion | flops 15142748160 | bytes 29982720 | tf_op jit(solution)/shard_map/tk,dk->td/dot_general | solution.py:180
  1222.8 22.8 %psum.89 = bf16[1280]{0:T(1024)(128)(2,1)S(1)} all-reduce(bf16[1280]{0:T(1024)(128)(2,1)S(1)} %copy-done.37), channel_id=1, replica_groups=mesh['dp'=8,'mp'=4] {'dp'}, use_global_device_ids=true, to_apply=%region_19.20 | all-reduce | flops 1280 | bytes 5120 | tf_op jit(solution)/shard_map/psum | solution.py:195
  1248.3 263.4 %all-reduce.4.cloned.1.call-done = (bf16[1280,320]{0,1:T(8,128)(2,1)}, bf16[1280,320]{0,1:T(8,128)(2,1)}, bf16[1280,320]{0,1:T(8,128)(2,1)}, bf16[320,1280]{1,0:...) async-done(((bf16[1280,320]{0,1:T(8,128)(2,1)}, bf16[1280,320]{0,1:T(8,128)(2,1)}, bf16[1280,320]{0,1:T(8,128)(2,1)}, bf16[320,1280]{1,0:T(8,128)(2,1)}, ...) | async-done | bytes 9830416 | tf_op jit(solution)/shard_map/psum | solution.py:190
  1529.6 103.7 %reduce-scatter.11.cloned.1.call-done = bf16[1536,1280]{1,0:T(8,128)(2,1)} async-done(((bf16[6144,1280]{1,0:T(8,128)(2,1)}), bf16[1536,1280]{1,0:T(8,128)(2,1)}) %reduce-scatter.11.cloned.1.call-update) | async-done | bytes 3932176 | tf_op jit(solution)/shard_map/reduce_scatter | solution.py:179
  1651.3 40.0 %all-reduce = (f32[1280]{0:T(1024)}, f32[1280]{0:T(1024)}, f32[1280]{0:T(1024)}, f32[3]{0:T(128)S(1)}, f32[]{:T(128)}) all-reduce(f32[1280]{0:T(1024)S(1)} %get-tuple-element.37, f32[1280]{0:T(1024)S(1)} %get-tuple-element.16, f32[1280]{0:T(1024)S(1)} %copy-done.32, ...), channel_id=1, replica_groups=mesh['dp'=8,'mp'=4] {'dp','mp'}, use_global_device_ids=true, to_apply=%region_22.23 | all-reduce | flops 3844 | bytes 30752 | tf_op jit(solution)/shard_map/psum | solution.py:198
  (166 shorter events, 361.5 us)
Async XLA Ops:
  7.2 507.9 %copy-start = (bf16[1280,1280]{1,0:T(8,128)(2,1)S(1)}, bf16[1280,1280]{1,0:T(8,128)(2,1)}, u32[]{:S(2)}) copy-start(bf16[1280,1280]{1,0:T(8,128)(2,1)} %param.20) | copy-start | bytes 9830404
  7.2 112.4 %all-gather.5.cloned.1.call-start = ((), (), s32[]{:S(2)}) async-start(), calls=%async_computation.4 | async-start | bytes 19660800 | tf_op jit(solution)/shard_map/all_gather | solution.py:67
  16.8 389.4 %reduce-scatter.5.cloned.1.call-start = ((), (), s32[]{:S(2)}) async-start(), calls=%async_computation.5 | async-start | bytes 19660800 | tf_op jit(solution)/shard_map/reduce_scatter | solution.py:88
  17.4 121.3 %copy-start.18 = (s32[96,64]{0,1:T(8,128)}, s32[96,64]{0,1:T(8,128)S(1)}, u32[]{:S(2)}) copy-start(s32[96,64]{0,1:T(8,128)S(1)} %convert_reduce_fusion.1) | copy-start | bytes 73732
  286.2 228.8 %all-gather.7.cloned.1.call-start = ((), (), s32[]{:S(2)}) async-start(), calls=%async_computation.6 | async-start | bytes 19660800 | tf_op jit(solution)/shard_map/all_gather | solution.py:96
  286.9 128.0 %copy-start.20 = (f32[1280]{0:T(1024)}, f32[1280]{0:T(1024)S(1)}, u32[]{:S(2)}) copy-start(f32[1280]{0:T(1024)S(1)} %convert_element_type.159) | copy-start | bytes 15364
  415.0 201.5 %all-gather.9.cloned.1.call-start = ((), (), s32[]{:S(2)}) async-start(), calls=%async_computation.8 | async-start | bytes 19660800 | tf_op jit(solution)/shard_map/all_gather | solution.py:120
  415.5 323.3 %reduce-scatter.7.cloned.1.call-start = ((), (), s32[]{:S(2)}) async-start(), calls=%async_computation.7 | async-start | bytes 19660800 | tf_op jit(solution)/shard_map/reduce_scatter | solution.py:102
  515.1 32.9 %copy-start.38 = (bf16[1280,1280]{1,0:T(8,128)(2,1)S(1)}, bf16[1280,1280]{1,0:T(8,128)(2,1)}, u32[]{:S(2)}) copy-start(bf16[1280,1280]{1,0:T(8,128)(2,1)} %param.22) | copy-start | bytes 9830404
  573.9 287.3 %reduce-scatter.9.cloned.1.call-start = ((), (), s32[]{:S(2)}) async-start(), calls=%async_computation.9 | async-start | bytes 19660800 | tf_op jit(solution)/shard_map/reduce_scatter | solution.py:129
  680.9 180.3 %copy-start.21 = (f32[1280]{0:T(1024)S(1)}, f32[1280]{0:T(1024)}, u32[]{:S(2)}) copy-start(f32[1280]{0:T(1024)} %copy-done.20) | copy-start | bytes 15364
  680.9 180.3 %copy-start.24 = (f32[1536]{0:T(1024)S(1)}, f32[1536]{0:T(1024)}, u32[]{:S(2)}) copy-start(f32[1536]{0:T(1024)} %copy-done.23) | copy-start | bytes 18436
  680.9 299.8 %all-gather.11.cloned.1.call-start = ((), (), s32[]{:S(2)}) async-start(), calls=%async_computation.10 | async-start | bytes 19660800 | tf_op jit(solution)/shard_map/all_gather | solution.py:140
  861.2 14.1 copy-start.3
  861.2 14.1 copy-start.6
  880.6 631.1 %all-reduce.4.cloned.1.call-start = ((), (), s32[]{:S(2)}) async-start(), calls=%async_computation.12 | async-start | bytes 19660800 | tf_op jit(solution)/shard_map/psum | solution.py:190
  907.4 73.4 %copy-start.39 = (bf16[320,1280]{1,0:T(8,128)(2,1)S(1)}, bf16[320,1280]{1,0:T(8,128)(2,1)}, u32[]{:S(2)}) copy-start(bf16[320,1280]{1,0:T(8,128)(2,1)} %param.19) | copy-start | bytes 2457604
  1198.9 434.4 %reduce-scatter.11.cloned.1.call-start = ((), (), s32[]{:S(2)}) async-start(), calls=%async_computation.11 | async-start | bytes 19660800 | tf_op jit(solution)/shard_map/reduce_scatter | solution.py:179
  1520.5 112.8 %copy-start.27 = (f32[1280]{0:T(1024)S(1)}, f32[1280]{0:T(1024)}, u32[]{:S(2)}) copy-start(f32[1280]{0:T(1024)} %copy-done.26) | copy-start | bytes 15364
  1520.5 112.8 %copy-start.29 = (f32[1536]{0:T(1024)S(1)}, f32[1536]{0:T(1024)}, u32[]{:S(2)}) copy-start(f32[1536]{0:T(1024)} %copy-done.28) | copy-start | bytes 18436
  1525.1 113.8 %copy-start.22 = (f32[1280]{0:T(1024)S(1)}, f32[1280]{0:T(1024)}, u32[]{:S(2)}) copy-start(f32[1280]{0:T(1024)} %copy-done.20) | copy-start | bytes 15364
  1525.1 113.8 %copy-start.25 = (f32[1536]{0:T(1024)S(1)}, f32[1536]{0:T(1024)}, u32[]{:S(2)}) copy-start(f32[1536]{0:T(1024)} %copy-done.23) | copy-start | bytes 18436
  1525.1 113.8 %copy-start.31 = (f32[1536]{0:T(1024)S(1)}, f32[1536]{0:T(1024)}, u32[]{:S(2)}) copy-start(f32[1536]{0:T(1024)} %copy-done.30) | copy-start | bytes 18436
  1638.9 53.6 %copy-start.1 = (bf16[1280,1280]{1,0:T(8,128)(2,1)S(1)}, bf16[1280,1280]{1,0:T(8,128)(2,1)}, u32[]{:S(2)}) copy-start(bf16[1280,1280]{1,0:T(8,128)(2,1)} %param.20) | copy-start | bytes 9830404
  (27 other events, 173.8 us)
Sparse Core Ops, SparseCore 0:
  16.9 102.6 all-gather.4
  286.4 119.8 reduce-scatter.4
  415.1 99.9 all-gather.6
  516.5 99.9 all-gather.8
  618.9 119.8 reduce-scatter.6
  741.3 119.8 reduce-scatter.8
  880.7 99.9 all-gather.10
  1199.0 312.5 all-reduce.3
  1514.5 118.8 reduce-scatter.10
where the time goes:
time: 1710 us; the launch traced here: 1700 us
  waiting for transfers between devices  948 us (55%)
  matrix products  346 us (20%)
  local copies, waits for them, and re-layouts  229 us (13%)
  other arithmetic  98.5 us (6%)
  blocking collectives  62.8 us (4%)
    psum x1, waiting for transfers between devices, per_device(): lax.psum(query_part.astype(jnp.bfloat16), 'dp').astype(jnp.float32)  263 us
    reduce_scatter x1, waiting for transfers between devices, per_device(): lax.psum_scatter(jnp.einsum('tf,df->td', preact_grad, up_weight, preferre...  122 us
    reduce_scatter x1, waiting for transfers between devices, per_device(): lax.psum_scatter(jnp.dot(mixed, out_weight, preferred_element_type=jnp.fl...  119 us
    reduce_scatter x1, waiting for transfers between devices, per_device(): lax.psum_scatter(jnp.einsum('tk,dk->td', joined_grad, joined_weight, pref...  104 us
    all_gather x1, waiting for transfers between devices, per_device(): second_rows = lax.all_gather(second_normed, 'mp', axis=0, tiled=True)  99.5 us
    all_gather x1, waiting for transfers between devices, per_device(): first_rows = lax.all_gather(first_normed, 'mp', axis=0, tiled=True)  93.2 us
    reduce_scatter x1, waiting for transfers between devices, per_device(): lax.psum_scatter(jnp.dot(active, down_weight, preferred_element_type=jnp....  56.3 us
    all_gather x1, waiting for transfers between devices, per_device(): branch_grad = lax.all_gather(branch_low, 'mp', axis=0, tiled=True)  46.6 us
  transfers between devices with their start and end apart: 9, of which 9 were waited for; matrix products, arithmetic and copies ran while one was open for 14% of the time, Pallas kernels for 0%

commit v1 on v0

--- a/solution.py
+++ b/solution.py
@@ -137,7 +137,16 @@
     second_gain_part, second_back = norm_back(hidden, second_scale, second_gain, second_grad)
     hidden_grad = grad_out + second_back
     branch_low = hidden_grad.astype(jnp.bfloat16)
-    branch_grad = lax.all_gather(branch_low, "mp", axis=0, tiled=True)
+    ways = lax.axis_size("mp")
+    up = [(d, (d + 1) % ways) for d in range(ways)]
+    down = [(d, (d - 1) % ways) for d in range(ways)]
+    earlier, later = ([branch_low], [branch_low])
+    for _ in range(ways // 2):
+        earlier.append(lax.ppermute(earlier[-1], "mp", up))
+    for _ in range((ways - 1) // 2):
+        later.append(lax.ppermute(later[-1], "mp", down))
+    line = jnp.concatenate([*earlier[::-1], *later[1:]], axis=0)
+    branch_grad = jnp.roll(line, (lax.axis_index("mp") - ways // 2) * branch_low.shape[0], axis=0)
     out_part = jnp.einsum("tk,td->kd", mixed, branch_grad, preferred_element_type=jnp.float32)
     mixed_grad = jnp.einsum(
         "td,kd->tk", branch_grad, out_weight, preferred_element_type=jnp.float32

time: 1710 us -> 1750 us (1.023)
  local copies, waits for them, and re-layouts: 229 us -> 255 us
  waiting for transfers between devices: 948 us -> 968 us
    ppermute x0 -> x3, waiting for transfers between devices: none -> 64.9 us  [the longest x2 50.3 us: per_device(): earlier.append(lax.ppermute(earlier[-1], 'mp', up))]
    all_gather x1 -> x0, waiting for transfers between devices: 46.6 us -> none  [per_device(): branch_grad = lax.all_gather(branch_low, 'mp', axis=0, tiled=True)]
    unnamed x87 -> x98, local copies, waits for them, and re-layouts: 10.5 us -> 34.3 us
  transfers between devices with their start and end apart: 9 -> 11, of which waited for: 9 -> 11; matrix products, arithmetic and copies ran while one was open for 14% -> 14% of each run, Pallas kernels for 0% -> 0%
where the time goes in v1:
time: 1750 us; the launch traced here: 1740 us
  waiting for transfers between devices  968 us (55%)
  matrix products  343 us (20%)
  local copies, waits for them, and re-layouts  255 us (15%)
  other arithmetic  98.1 us (6%)
  blocking collectives  63 us (4%)
    psum x1, waiting for transfers between devices, per_device(): lax.psum(query_part.astype(jnp.bfloat16), 'dp').astype(jnp.float32)  265 us
    reduce_scatter x1, waiting for transfers between devices, per_device(): lax.psum_scatter(jnp.einsum('tf,df->td', preact_grad, up_weight, preferre...  122 us
    reduce_scatter x1, waiting for transfers between devices, per_device(): lax.psum_scatter(jnp.dot(mixed, out_weight, preferred_element_type=jnp.fl...  119 us
    reduce_scatter x1, waiting for transfers between devices, per_device(): lax.psum_scatter(jnp.einsum('tk,dk->td', joined_grad, joined_weight, pref...  104 us
    all_gather x1, waiting for transfers between devices, per_device(): second_rows = lax.all_gather(second_normed, 'mp', axis=0, tiled=True)  99.5 us
    all_gather x1, waiting for transfers between devices, per_device(): first_rows = lax.all_gather(first_normed, 'mp', axis=0, tiled=True)  93.4 us
    reduce_scatter x1, waiting for transfers between devices, per_device(): lax.psum_scatter(jnp.dot(active, down_weight, preferred_element_type=jnp....  56.3 us
    ppermute x2, waiting for transfers between devices, per_device(): earlier.append(lax.ppermute(earlier[-1], 'mp', up))  50.3 us
  transfers between devices with their start and end apart: 11, of which 11 were waited for; matrix products, arithmetic and copies ran while one was open for 14% of the time, Pallas kernels for 0%

profile of v1, /device:TPU:0, one launch (start us, length us, event | category | flops | bytes accessed | tf_op | source)
XLA Modules:
  0.0 1744.8 jit_solution(16346501392932742059)
XLA Ops:
  26.2 93.4 %all-gather.4.cloned.1.call-done = bf16[6144,1280]{1,0:T(8,128)(2,1)} async-done(((bf16[1536,1280]{1,0:T(8,128)(2,1)}), bf16[6144,1280]{1,0:T(8,128)(2,1)}) %all-gather.4.cloned.1.call-update) | async-done | bytes 15728656 | tf_op jit(solution)/shard_map/all_gather | solution.py:67
  119.7 19.1 %convolution_convert_fusion.5 = bf16[6144,960]{0,1:T(8,128)(2,1)S(1)} fusion(bf16[6144,1280]{1,0:T(8,128)(2,1)} %all-gather.4.cloned.1.call-done, bf16[1280,960]{0,1:T(8,128)(2,1)} %constant_dynamic-update-slice_fusion), kind=kOutput, calls=%fused_computation.29 | convolution fusion | flops 15105392640 | bytes 29982720 | tf_op jit(solution)/shard_map/dot_general | solution.py:69
  243.7 18.5 %copy.67 = bf16[96,64,4,80]{3,2,1,0:T(4,128)(2,1)} copy(bf16[96,64,4,80]{3,1,2,0:T(8,128)(2,1)} %convert_bitcast_fusion.1) | data formatting | bytes 7864320 | tf_op jit(solution)/shard_map/convert_element_type | solution.py:87
  287.2 119.3 %reduce-scatter.5.cloned.1.call-done = bf16[1536,1280]{1,0:T(8,128)(2,1)} async-done(((bf16[6144,1280]{1,0:T(8,128)(2,1)}), bf16[1536,1280]{1,0:T(8,128)(2,1)}) %reduce-scatter.5.cloned.1.call-update) | async-done | bytes 3932176 | tf_op jit(solution)/shard_map/reduce_scatter | solution.py:88
  415.9 99.5 %all-gather.6.cloned.1.call-done = bf16[6144,1280]{1,0:T(8,128)(2,1)} async-done(((bf16[1536,1280]{1,0:T(8,128)(2,1)}), bf16[6144,1280]{1,0:T(8,128)(2,1)}) %all-gather.6.cloned.1.call-update) | async-done | bytes 15728656 | tf_op jit(solution)/shard_map/all_gather | solution.py:96
  515.4 32.7 %fusion = (bf16[6144,1280]{1,0:T(8,128)(2,1)}, f32[6144,1280]{1,0:T(8,128)}) fusion(f32[1280]{0:T(1024)S(1)} %convert_element_type.161, bf16[6144,1280]{1,0:T(8,128)(2,1)} %all-gather.6.cloned.1.call-done, bf16[1280,1280]{1,0:T(8,128)(2,1)S(1)} %copy-done), kind=kOutput, calls=%fused_computation.3 | convolution fusion | flops 20179845120 | bytes 66196480 | tf_op jit(solution)/shard_map/dot_general | solution.py:97
  548.1 25.9 %convolution_convert_fusion.2 = bf16[6144,1280]{1,0:T(8,128)(2,1)} fusion(bf16[6144,1280]{1,0:T(8,128)(2,1)} %get-tuple-element.44, bf16[1280,1280]{1,0:T(8,128)(2,1)S(1)} %copy-done.38), kind=kOutput, calls=%fused_computation.6 | convolution fusion | flops 20140523520 | bytes 34734080 | tf_op jit(solution)/shard_map/dot_general | solution.py:103
  574.1 42.7 %all-gather.8.cloned.1.call-done = bf16[6144,1280]{1,0:T(8,128)(2,1)} async-done(((bf16[1536,1280]{1,0:T(8,128)(2,1)}), bf16[6144,1280]{1,0:T(8,128)(2,1)}) %all-gather.8.cloned.1.call-update) | async-done | bytes 15728656 | tf_op jit(solution)/shard_map/all_gather | solution.py:120
  616.8 38.5 %fusion.51 = (bf16[1280]{0:T(1024)(128)(2,1)}, bf16[6144,1280]{1,0:T(8,128)(2,1)}) fusion(f32[6144,1280]{1,0:T(8,128)} %get-tuple-element.45, f32[1280]{0:T(1024)S(1)} %convert_element_type.161, bf16[6144,1280]{1,0:T(8,128)(2,1)} %all-gather.8.cloned.1.call-done, bf16[1280,1280]{1,0:T(8,128)(2,1)} %param.22), kind=kOutput, calls=%fused_computation.103 | convolution fusion | flops 20234893312 | bytes 66199040 | tf_op jit(solution)/shard_map/td,fd->tf/dot_general | solution.py:122
  655.3 25.9 %convolution_convert_fusion = bf16[6144,1280]{1,0:T(8,128)(2,1)} fusion(bf16[6144,1280]{1,0:T(8,128)(2,1)} %get-tuple-element.49, bf16[1280,1280]{1,0:T(8,128)(2,1)S(1)} %copy-done), kind=kOutput, calls=%fused_computation.4 | convolution fusion | flops 20140523520 | bytes 34734080 | tf_op jit(solution)/shard_map/tf,df->td/dot_general | solution.py:130
  682.8 56.3 %reduce-scatter.7.cloned.1.call-done = bf16[1536,1280]{1,0:T(8,128)(2,1)} async-done(((bf16[6144,1280]{1,0:T(8,128)(2,1)}), bf16[1536,1280]{1,0:T(8,128)(2,1)}) %reduce-scatter.7.cloned.1.call-update) | async-done | bytes 3932176 | tf_op jit(solution)/shard_map/reduce_scatter | solution.py:102
  739.2 122.3 %reduce-scatter.9.cloned.1.call-done = bf16[1536,1280]{1,0:T(8,128)(2,1)} async-done(((bf16[6144,1280]{1,0:T(8,128)(2,1)}), bf16[1536,1280]{1,0:T(8,128)(2,1)}) %reduce-scatter.9.cloned.1.call-update) | async-done | bytes 3932176 | tf_op jit(solution)/shard_map/reduce_scatter | solution.py:129
  880.9 45.4 %collective-permute-done = bf16[1536,1280]{1,0:T(8,128)(2,1)} collective-permute-done((bf16[1536,1280]{1,0:T(8,128)(2,1)}, bf16[1536,1280]{1,0:T(8,128)(2,1)}, u32[]{:S(2)}, u32[]{:S(2)}) %collective-permute-start) | collective-permute-done | bytes 3932192 | tf_op jit(solution)/shard_map/ppermute | solution.py:145
  926.3 26.7 %convolution_convert_fusion.6 = bf16[1280,1280]{1,0:T(8,128)(2,1)} fusion(bf16[6144,1280]{1,0:T(8,128)(2,1)} %get-tuple-element.44, bf16[6144,1280]{1,0:T(8,128)(2,1)} %all-gather.8.cloned.1.call-done), kind=kOutput, calls=%fused_computation.63 | convolution fusion | flops 20134297600 | bytes 34734080 | tf_op jit(solution)/shard_map/tf,td->fd/dot_general | solution.py:121
  954.7 26.8 %convolution_convert_fusion.7 = bf16[1280,1280]{1,0:T(8,128)(2,1)} fusion(bf16[6144,1280]{1,0:T(8,128)(2,1)} %all-gather.6.cloned.1.call-done, bf16[6144,1280]{1,0:T(8,128)(2,1)} %get-tuple-element.49), kind=kOutput, calls=%fused_computation.64 | convolution fusion | flops 20134297600 | bytes 34734080 | tf_op jit(solution)/shard_map/td,tf->df/dot_general | solution.py:128
  1132.9 18.3 %copy.77 = bf16[96,64,4,80]{3,2,1,0:T(4,128)(2,1)} copy(bf16[96,64,4,80]{3,1,2,0:T(8,128)(2,1)} %convert_bitcast_fusion) | data formatting | bytes 7864320 | tf_op jit(solution)/shard_map/convert_element_type | solution.py:164
  1162.0 18.5 %copy.73 = bf16[96,64,4,80]{3,2,1,0:T(4,128)(2,1)} copy(bf16[96,64,4,80]{3,1,2,0:T(8,128)(2,1)} %fusion.33) | data formatting | bytes 7864320 | tf_op jit(solution)/shard_map/convert_element_type | solution.py:169
  1191.3 18.3 %copy.75 = bf16[96,64,4,80]{3,2,1,0:T(4,128)(2,1)} copy(bf16[96,64,4,80]{3,1,2,0:T(8,128)(2,1)} %fusion.34) | data formatting | bytes 7864320 | tf_op jit(solution)/shard_map/convert_element_type | solution.py:173
  1220.4 20.7 %fusion.37 = bf16[1280,960]{0,1:T(8,128)(2,1)S(1)} fusion(bf16[6144,1280]{1,0:T(8,128)(2,1)} %all-gather.4.cloned.1.call-done, bf16[6144,320]{1,0:T(8,128)(2,1)} %reshape.110, bf16[6144,320]{1,0:T(8,128)(2,1)} %reshape.109, bf16[6144,320]{1,0:T(8,128)(2,1)} %reshape.108), kind=kOutput, calls=%fused_computation.72 | convolution fusion | flops 15136112640 | bytes 29982720 | tf_op jit(solution)/shard_map/td,tk->dk/dot_general | solution.py:182
  1242.6 22.9 %convolution_convert_fusion.4 = bf16[6144,1280]{1,0:T(8,128)(2,1)} fusion(bf16[1280,960]{0,1:T(8,128)(2,1)} %constant_dynamic-update-slice_fusion, bf16[6144,320]{1,0:T(8,128)(2,1)} %reshape.110, bf16[6144,320]{1,0:T(8,128)(2,1)} %reshape.109, bf16[6144,320]{1,0:T(8,128)(2,1)} %reshape.108), kind=kOutput, calls=%fused_computation.8 | convolution fusion | flops 15142748160 | bytes 29982720 | tf_op jit(solution)/shard_map/tk,dk->td/dot_general | solution.py:189
  1266.3 23.0 %psum.89 = bf16[1280]{0:T(1024)(128)(2,1)S(1)} all-reduce(bf16[1280]{0:T(1024)(128)(2,1)S(1)} %copy-done.37), channel_id=1, replica_groups=mesh['dp'=8,'mp'=4] {'dp'}, use_global_device_ids=true, to_apply=%region_19.20 | all-reduce | flops 1280 | bytes 5120 | tf_op jit(solution)/shard_map/psum | solution.py:204
  1291.8 265.1 %all-reduce.4.cloned.1.call-done = (bf16[1280,320]{0,1:T(8,128)(2,1)}, bf16[1280,320]{0,1:T(8,128)(2,1)}, bf16[1280,320]{0,1:T(8,128)(2,1)}, bf16[320,1280]{1,0:...) async-done(((bf16[1280,320]{0,1:T(8,128)(2,1)}, bf16[1280,320]{0,1:T(8,128)(2,1)}, bf16[1280,320]{0,1:T(8,128)(2,1)}, bf16[320,1280]{1,0:T(8,128)(2,1)}, ...) | async-done | bytes 9830416 | tf_op jit(solution)/shard_map/psum | solution.py:199
  1574.9 103.7 %reduce-scatter.11.cloned.1.call-done = bf16[1536,1280]{1,0:T(8,128)(2,1)} async-done(((bf16[6144,1280]{1,0:T(8,128)(2,1)}), bf16[1536,1280]{1,0:T(8,128)(2,1)}) %reduce-scatter.11.cloned.1.call-update) | async-done | bytes 3932176 | tf_op jit(solution)/shard_map/reduce_scatter | solution.py:188
  1696.5 40.0 %all-reduce = (f32[1280]{0:T(1024)}, f32[1280]{0:T(1024)}, f32[1280]{0:T(1024)}, f32[3]{0:T(128)S(1)}, f32[]{:T(128)}) all-reduce(f32[1280]{0:T(1024)S(1)} %get-tuple-element.37, f32[1280]{0:T(1024)S(1)} %get-tuple-element.16, f32[1280]{0:T(1024)S(1)} %copy-done.32, ...), channel_id=1, replica_groups=mesh['dp'=8,'mp'=4] {'dp','mp'}, use_global_device_ids=true, to_apply=%region_22.23 | all-reduce | flops 3844 | bytes 30752 | tf_op jit(solution)/shard_map/psum | solution.py:207
  (182 shorter events, 405.7 us)
Async XLA Ops:
  7.2 508.2 %copy-start = (bf16[1280,1280]{1,0:T(8,128)(2,1)S(1)}, bf16[1280,1280]{1,0:T(8,128)(2,1)}, u32[]{:S(2)}) copy-start(bf16[1280,1280]{1,0:T(8,128)(2,1)} %param.20) | copy-start | bytes 9830404
  7.2 112.5 %all-gather.4.cloned.1.call-start = ((), (), s32[]{:S(2)}) async-start(), calls=%async_computation.4 | async-start | bytes 19660800 | tf_op jit(solution)/shard_map/all_gather | solution.py:67
  16.8 389.8 %reduce-scatter.5.cloned.1.call-start = ((), (), s32[]{:S(2)}) async-start(), calls=%async_computation.5 | async-start | bytes 19660800 | tf_op jit(solution)/shard_map/reduce_scatter | solution.py:88
  17.4 121.3 %copy-start.18 = (s32[96,64]{0,1:T(8,128)}, s32[96,64]{0,1:T(8,128)S(1)}, u32[]{:S(2)}) copy-start(s32[96,64]{0,1:T(8,128)S(1)} %convert_reduce_fusion.1) | copy-start | bytes 73732
  286.5 228.9 %all-gather.6.cloned.1.call-start = ((), (), s32[]{:S(2)}) async-start(), calls=%async_computation.6 | async-start | bytes 19660800 | tf_op jit(solution)/shard_map/all_gather | solution.py:96
  287.2 128.0 %copy-start.20 = (f32[1280]{0:T(1024)}, f32[1280]{0:T(1024)S(1)}, u32[]{:S(2)}) copy-start(f32[1280]{0:T(1024)S(1)} %convert_element_type.159) | copy-start | bytes 15364
  415.3 201.5 %all-gather.8.cloned.1.call-start = ((), (), s32[]{:S(2)}) async-start(), calls=%async_computation.8 | async-start | bytes 19660800 | tf_op jit(solution)/shard_map/all_gather | solution.py:120
  415.9 323.3 %reduce-scatter.7.cloned.1.call-start = ((), (), s32[]{:S(2)}) async-start(), calls=%async_computation.7 | async-start | bytes 19660800 | tf_op jit(solution)/shard_map/reduce_scatter | solution.py:102
  515.4 32.7 %copy-start.38 = (bf16[1280,1280]{1,0:T(8,128)(2,1)S(1)}, bf16[1280,1280]{1,0:T(8,128)(2,1)}, u32[]{:S(2)}) copy-start(bf16[1280,1280]{1,0:T(8,128)(2,1)} %param.22) | copy-start | bytes 9830404
  574.1 287.4 %reduce-scatter.9.cloned.1.call-start = ((), (), s32[]{:S(2)}) async-start(), calls=%async_computation.9 | async-start | bytes 19660800 | tf_op jit(solution)/shard_map/reduce_scatter | solution.py:129
  681.2 180.3 %copy-start.21 = (f32[1280]{0:T(1024)S(1)}, f32[1280]{0:T(1024)}, u32[]{:S(2)}) copy-start(f32[1280]{0:T(1024)} %copy-done.20) | copy-start | bytes 15364
  681.2 180.3 %copy-start.24 = (f32[1536]{0:T(1024)S(1)}, f32[1536]{0:T(1024)}, u32[]{:S(2)}) copy-start(f32[1536]{0:T(1024)} %copy-done.23) | copy-start | bytes 18436
  681.3 875.7 %all-reduce.4.cloned.1.call-start = ((), (), s32[]{:S(2)}) async-start(), calls=%async_computation.11 | async-start | bytes 19660800 | tf_op jit(solution)/shard_map/psum | solution.py:199
  861.5 14.0 copy-start.6
  880.9 45.4 %collective-permute-start = (bf16[1536,1280]{1,0:T(8,128)(2,1)}, bf16[1536,1280]{1,0:T(8,128)(2,1)}, u32[]{:S(2)}, u32[]{:S(2)}) collective-permute-start(bf16[1536,1280]{1,0:T(8,128)(2,1)} %fusion.47), channel_id=1, source_target_pairs={{0,1},{1,2},{2,3},{3,0},{4,5},{5,6},{6,7},{7,4},{8,9},{9,10},{10,1... | collective-permute-start | bytes 11796488 | tf_op jit(solution)/shard_map/ppermute | solution.py:145
  926.3 60.1 %collective-permute-start.1 = (bf16[1536,1280]{1,0:T(8,128)(2,1)}, bf16[1536,1280]{1,0:T(8,128)(2,1)S(1)}, u32[]{:S(2)}, u32[]{:S(2)}) collective-permute-start(bf16[1536,1280]{1,0:T(8,128)(2,1)} %collective-permute-done), channel_id=1, source_target_pairs={{0,1},{1,2},{2,3},{3,0},{4,5},{5,6},{6,7},{7,4},{8,9},{9,10},{10,1... | collective-permute-start | bytes 11796488 | tf_op jit(solution)/shard_map/ppermute | solution.py:145
  953.0 58.7 %collective-permute-start.2 = (bf16[1536,1280]{1,0:T(8,128)(2,1)}, bf16[1536,1280]{1,0:T(8,128)(2,1)S(1)}, u32[]{:S(2)}, u32[]{:S(2)}) collective-permute-start(bf16[1536,1280]{1,0:T(8,128)(2,1)} %fusion.47), channel_id=1, source_target_pairs={{0,3},{1,0},{2,1},{3,2},{4,7},{5,4},{6,5},{7,6},{8,11},{9,8},{10,9... | collective-permute-start | bytes 11796488 | tf_op jit(solution)/shard_map/ppermute | solution.py:147
  1242.6 436.0 %reduce-scatter.11.cloned.1.call-start = ((), (), s32[]{:S(2)}) async-start(), calls=%async_computation.10 | async-start | bytes 19660800 | tf_op jit(solution)/shard_map/reduce_scatter | solution.py:188
  1565.8 112.8 %copy-start.27 = (f32[1280]{0:T(1024)S(1)}, f32[1280]{0:T(1024)}, u32[]{:S(2)}) copy-start(f32[1280]{0:T(1024)} %copy-done.26) | copy-start | bytes 15364
  1565.8 112.8 %copy-start.29 = (f32[1536]{0:T(1024)S(1)}, f32[1536]{0:T(1024)}, u32[]{:S(2)}) copy-start(f32[1536]{0:T(1024)} %copy-done.28) | copy-start | bytes 18436
  1570.3 113.8 %copy-start.22 = (f32[1280]{0:T(1024)S(1)}, f32[1280]{0:T(1024)}, u32[]{:S(2)}) copy-start(f32[1280]{0:T(1024)} %copy-done.20) | copy-start | bytes 15364
  1570.3 113.8 %copy-start.25 = (f32[1536]{0:T(1024)S(1)}, f32[1536]{0:T(1024)}, u32[]{:S(2)}) copy-start(f32[1536]{0:T(1024)} %copy-done.23) | copy-start | bytes 18436
  1570.3 113.8 %copy-start.31 = (f32[1536]{0:T(1024)S(1)}, f32[1536]{0:T(1024)}, u32[]{:S(2)}) copy-start(f32[1536]{0:T(1024)} %copy-done.30) | copy-start | bytes 18436
  1684.1 53.6 %copy-start.1 = (bf16[1280,1280]{1,0:T(8,128)(2,1)S(1)}, bf16[1280,1280]{1,0:T(8,128)(2,1)}, u32[]{:S(2)}) copy-start(bf16[1280,1280]{1,0:T(8,128)(2,1)} %param.20) | copy-start | bytes 9830404
  (31 other events, 206.9 us)
Sparse Core Ops, SparseCore 0:
  16.9 102.6 all-gather.3
  286.7 119.8 reduce-scatter.4
  415.4 99.9 all-gather.5
  516.8 99.9 all-gather.7
  619.3 119.8 reduce-scatter.6
  741.6 119.8 reduce-scatter.8
  1242.7 314.1 all-reduce.3
  1559.7 118.8 reduce-scatter.10
